TPU v7x, 32 devices: a whole 2x2x4 slice. The times are simulated.
32 devices in a mesh: dp: 2 (over x), expert: 4 (over y, core), mp: 4 (over z).
Axes of the slice: x: 2, y: 2, z: 4, core: 2. Of those that a mesh axis runs over, the one named last changes fastest.
Arguments:
- tokens: bfloat16 [128, 3072], P('dp'), may hold values from -6 to 6
- expert_ids: int32 [128, 2], P('dp'), may hold values from 0 to 3, all different within a row; in each aligned block of 64 rows (0 to 63, 64 to 127, ...) at most 64 rows name the same one
- gate_values: float32 [128, 2], P('dp'), may hold values from 0.2 to 1
- targets: int32 [128], P('dp'), may hold values from 0 to 32767
- w_gate: bfloat16 [4, 3072, 4, 2048], P('expert', None, 'mp', 'dp'), may hold values from -0.109375 to 0.109375
- w_up: bfloat16 [4, 3072, 4, 2048], P('expert', None, 'mp', 'dp'), may hold values from -0.109375 to 0.109375
- w_down: bfloat16 [4, 4, 2048, 3072], P('expert', 'mp', None, 'dp'), may hold values from -0.0625 to 0.0625
- norm_gain: float32 [3072], replicated, may hold values from 0.1 to 1.9
- lens_head: bfloat16 [3072, 32768], P('dp', ('expert', 'mp')), may hold values from -120 to 120
Outputs:
- mixed: bfloat16 [128, 3072], P('dp')
- log_probs: float32 [128], P('dp')
Inputs may be any that keep to these rules, and one draw needn't show every extreme that they name: `expert_ids`: each row names two different experts; in each aligned block of 64 rows no expert is named by more than 64 rows, a bound that some block reaches.
All inputs are finite; a program needn't handle non-finite values.
Results may differ from a plain program's by a relative error of at most 0.0041.
Values may be sent and summed in bfloat16 or wider, within the bound.
A program may use at most 128 MiB of HBM per device.

v0:
```python
import jax
import jax.numpy as jnp
from jax import lax
from jax.sharding import PartitionSpec as P


def per_device(
    tokens, expert_ids, gate_values, targets, w_gate, w_up, w_down, norm_gain, lens_head
):
    row_count = tokens.shape[0]
    feat_count = tokens.shape[1]
    owner = lax.axis_index("expert")
    capacity = min(row_count, 4 * row_count // lax.axis_size("expert"))
    matches = expert_ids == owner
    chosen = jnp.any(matches, axis=1)
    weights = jnp.sum(jnp.where(matches, gate_values, jnp.float32(0.0)), axis=1)
    position = jnp.cumsum(chosen.astype(jnp.int32)) - 1
    slot_ids = lax.broadcasted_iota(jnp.int32, (capacity, row_count), 0)
    placing = (slot_ids == position[None, :]) & chosen[None, :]
    picker = placing.astype(jnp.bfloat16)
    picked = jnp.dot(picker, tokens, preferred_element_type=jnp.float32).astype(jnp.bfloat16)
    gate_mat = w_gate.reshape(feat_count, -1)
    up_mat = w_up.reshape(feat_count, -1)
    down_mat = w_down.reshape(w_down.shape[2], w_down.shape[3])
    shard_part = lax.all_gather(picked, "dp", axis=0, tiled=True)
    gate_part = jnp.dot(shard_part, gate_mat, preferred_element_type=jnp.float32)
    up_part = jnp.dot(shard_part, up_mat, preferred_element_type=jnp.float32)
    hidden = (jax.nn.silu(gate_part) * up_part).astype(jnp.bfloat16)
    partial_value = jnp.dot(
        lax.all_gather(hidden, "dp", axis=1, tiled=True),
        down_mat,
        preferred_element_type=jnp.float32,
    )
    expert_out = lax.psum(partial_value, "mp").astype(jnp.bfloat16)
    returned = lax.all_to_all(expert_out, "dp", split_axis=0, concat_axis=1, tiled=True)
    spread_w = placing.astype(jnp.float32) * weights[None, :]
    contrib = lax.dot_general(
        spread_w,
        returned.astype(jnp.float32),
        (((0,), (0,)), ((), ())),
        precision=lax.Precision.HIGHEST,
    )
    summed = lax.psum(contrib, "expert")
    mixed = (tokens.astype(jnp.float32) + summed).astype(jnp.bfloat16)
    mixed_f = mixed.astype(jnp.float32)
    scale = lax.rsqrt(jnp.mean(mixed_f * mixed_f, axis=1, keepdims=True) + 1e-05)
    normed = (mixed_f * scale * norm_gain[None, :]).astype(jnp.bfloat16)
    vocab_cols = lens_head.shape[1]
    vocab_start = (
        lax.axis_index("expert") * lax.axis_size("mp") + lax.axis_index("mp")
    ) * vocab_cols
    logits = jnp.dot(
        normed,
        lax.all_gather(lens_head, "dp", axis=0, tiled=True),
        preferred_element_type=jnp.float32,
    )
    columns = vocab_start + lax.broadcasted_iota(jnp.int32, (1, vocab_cols), 1)
    target_hit = columns == targets[:, None]
    target_local = jnp.sum(jnp.where(target_hit, logits, jnp.float32(0.0)), axis=1)
    local_top = jnp.max(logits, axis=1)
    global_top = lax.pmax(local_top, ("expert", "mp"))
    local_total = jnp.sum(jnp.exp(logits - global_top[:, None]), axis=1)
    exp_total, target_logit = lax.psum((local_total, target_local), ("expert", "mp"))
    log_probs = target_logit - global_top - jnp.log(exp_total)
    return (mixed, log_probs)


def solution(mesh):
    in_specs = (
        P("dp", None),
        P("dp", None),
        P("dp", None),
        P("dp"),
        P("expert", None, "mp", "dp"),
        P("expert", None, "mp", "dp"),
        P("expert", "mp", None, "dp"),
        P(),
        P("dp", ("expert", "mp")),
    )
    out_specs = (P("dp", None), P("dp"))
    return jax.shard_map(
        per_device, mesh=mesh, in_specs=in_specs, out_specs=out_specs, check_vma=False
    )
```

profile of v0, /device:TPU:0, one launch (start us, length us, event | category | flops | bytes accessed | tf_op | source)
XLA Modules:
  0.0 313.7 jit_solution(13185323935273320964)
XLA Ops:
  8.0 0.7 fusion.31
  8.7 0.1 copy.14
  8.8 0.1 reduce-window.8
  8.9 0.1 add_reduce_fusion
  9.0 0.0 slice-start.2
  9.0 1.4 convolution_convert_fusion
  10.4 12.7 %all_gather.9 = bf16[128,3072]{1,0:T(8,128)(2,1)S(1)} all-gather(bf16[64,3072]{1,0:T(8,128)(2,1)S(1)} %convolution_convert_fusion), channel_id=1, replica_groups=mesh['dp'=2,'expert'=4,'mp'=4] {'dp'}, dimensions={0}, use_global_device_ids=true | all-gather | bytes 1179648 | tf_op jit(solution)/shard_map/all_gather | solution.py:25
  23.2 4.0 %fusion.4 = f32[128,1024]{1,0:T(8,128)S(1)} fusion(bf16[128,3072]{1,0:T(8,128)(2,1)S(1)} %all_gather.9, bf16[1,3072,1,1024]{3,1,2,0:T(8,128)(2,1)} %param.13), kind=kOutput, calls=%fused_computation.4 | convolution fusion | flops 805306368 | bytes 7602176 | tf_op jit(solution)/shard_map/dot_general | solution.py:26
  27.2 0.0 slice-start.1
  27.2 1.1 fusion.9
  28.3 8.2 %all_gather.10 = bf16[128,2048]{1,0:T(8,128)(2,1)S(1)} all-gather(bf16[128,1024]{1,0:T(8,128)(2,1)S(1)} %fusion.9), channel_id=1, replica_groups=mesh['dp'=2,'expert'=4,'mp'=4] {'dp'}, dimensions={1}, use_global_device_ids=true | all-gather | bytes 786432 | tf_op jit(solution)/shard_map/all_gather | solution.py:30
  36.4 0.0 copy-start.4
  36.5 1.0 fusion
  37.5 0.0 copy-start.1
  37.5 0.0 copy-start.2
  37.5 35.0 %all-reduce.5 = bf16[128,1536]{1,0:T(8,128)(2,1)} all-reduce(f32[128,1536]{1,0:T(8,128)S(1)} %fusion), channel_id=1, replica_groups=mesh['dp'=2,'expert'=4,'mp'=4] {'mp'}, use_global_device_ids=true, to_apply=%region_3.4 | all-reduce | flops 196608 | bytes 1179648 | tf_op jit(solution)/shard_map/psum | solution.py:34
  72.5 3.5 %all-to-all-start = ((bf16[2,64,1536]{2,1,0:T(8,128)(2,1)}), bf16[2,64,1536]{2,1,0:T(8,128)(2,1)S(1)}, u32[]{:S(2)}, u32[]{:S(2)}) async-start(bf16[2,64,1536]{2,1,0:T(8,128)(2,1)} %bitcast.4), calls=%async_computation | async-start | bytes 786432 | tf_op jit(solution)/shard_map/all_to_all | solution.py:35
  76.0 0.0 all-reduce.4.cloned.1.call-start
  76.1 5.8 %all-to-all-done = bf16[2,64,1536]{2,1,0:T(8,128)(2,1)S(1)} async-done(((bf16[2,64,1536]{2,1,0:T(8,128)(2,1)}), bf16[2,64,1536]{2,1,0:T(8,128)(2,1)S(1)}, u32[]{:S(2)}, u32[]{:S(2)}) %all-to-all-start) | async-done | bytes 393248 | tf_op jit(solution)/shard_map/all_to_all | solution.py:35
  81.9 1.4 fusion.19
  83.3 0.0 all-reduce.4.cloned.1.call-update
  83.3 0.0 all-gather.2.cloned.1.call-start
  83.4 0.5 all-gather.2.cloned.1.call-update
  83.9 32.0 %all-reduce.4.cloned.1.call-done = f32[64,3072]{1,0:T(8,128)} async-done(((f32[64,3072]{1,0:T(8,128)}), f32[64,3072]{1,0:T(8,128)}) %all-reduce.4.cloned.1.call-update) | async-done | bytes 786448 | tf_op jit(solution)/shard_map/psum | solution.py:43
  116.0 1.3 fusion.12
  117.3 0.0 copy-start
  117.3 118.1 %all-gather.2.cloned.1.call-done = bf16[3072,2048]{1,0:T(8,128)(2,1)} async-done(((bf16[1536,2048]{1,0:T(8,128)(2,1)}), bf16[3072,2048]{1,0:T(8,128)(2,1)}) %all-gather.2.cloned.1.call-update) | async-done | bytes 12582928 | tf_op jit(solution)/shard_map/all_gather | solution.py:54
  235.5 7.0 %fusion.32 = (f32[64]{0:T(128)S(1)}, f32[64,2048]{1,0:T(8,128)S(1)}) fusion(bf16[3072,2048]{1,0:T(8,128)(2,1)} %all-gather.2.cloned.1.call-done, bf16[64,3072]{1,0:T(8,128)(2,1)S(1)} %get-tuple-element.7, f32[3072]{0:T(1024)S(1)} %copy-done.2, f32[64]{0:T(128)S(1)} %add_rsqrt_fusion), kind=kOutput, calls=%fused_computation.39 | convolution fusion | flops 806223808 | bytes 13513216 | tf_op jit(solution)/shard_map/dot_general | solution.py:52
  242.5 33.2 %pmax.7 = f32[64]{0:T(128)S(1)} all-reduce(f32[64]{0:T(128)S(1)} %get-tuple-element.8), channel_id=1, replica_groups=mesh['dp'=2,'expert'=4,'mp'=4] {'expert','mp'}, use_global_device_ids=true, to_apply=%region_9.10 | all-reduce | flops 64 | bytes 512 | tf_op jit(solution)/shard_map/pmax | solution.py:61
  275.8 0.3 select_reduce_fusion
  276.0 29.7 %all-reduce = (f32[64]{0:T(128)S(1)}, f32[64]{0:T(128)S(1)}) all-reduce(f32[64]{0:T(128)S(1)} %get-tuple-element.3, f32[64]{0:T(128)S(1)} %get-tuple-element.2), channel_id=1, replica_groups=mesh['dp'=2,'expert'=4,'mp'=4] {'expert','mp'}, use_global_device_ids=true, to_apply=%region_11.12 | all-reduce | flops 128 | bytes 1024 | tf_op jit(solution)/shard_map/psum | solution.py:63
  305.7 0.5 log_subtract_fusion
  (21 shorter events, 0.1 us)
Async XLA Ops:
  9.0 18.1 %slice-start.2 = ((s8[6291456]{0:T(1024)(128)(4,1)}), s8[4194304]{0:T(1024)(128)(4,1)S(1)}, s32[]{:S(2)}) async-start(s8[6291456]{0:T(1024)(128)(4,1)} %bitcast.29), calls=%async_computation.5 | async-start | bytes 8388608
  23.2 4.0 %slice-start.3 = ((s8[6291456]{0:T(1024)(128)(4,1)}), s8[2097152]{0:T(1024)(128)(4,1)S(1)}, s32[]{:S(2)}) async-start(s8[6291456]{0:T(1024)(128)(4,1)} %bitcast.29), calls=%async_computation.6 | async-start | bytes 4194304
  23.2 13.3 %slice-start = ((s8[6291456]{0:T(1024)(128)(4,1)}), s8[4194304]{0:T(1024)(128)(4,1)S(1)}, s32[]{:S(2)}) async-start(s8[6291456]{0:T(1024)(128)(4,1)} %bitcast.25), calls=%async_computation.3 | async-start | bytes 8388608
  27.2 9.3 %slice-start.1 = ((s8[6291456]{0:T(1024)(128)(4,1)}), s8[2097152]{0:T(1024)(128)(4,1)S(1)}, s32[]{:S(2)}) async-start(s8[6291456]{0:T(1024)(128)(4,1)} %bitcast.25), calls=%async_computation.4 | async-start | bytes 4194304
  36.4 39.6 %copy-start.3 = (s32[64,2]{0,1:T(2,128)S(1)}, s32[64,2]{0,1:T(2,128)}, u32[]{:S(2)}) copy-start(s32[64,2]{0,1:T(2,128)} %param.10) | copy-start | bytes 1540
  36.4 39.6 %copy-start.4 = (f32[64,2]{0,1:T(2,128)S(1)}, f32[64,2]{0,1:T(2,128)}, u32[]{:S(2)}) copy-start(f32[64,2]{0,1:T(2,128)} %param.11) | copy-start | bytes 1540
  37.5 78.5 %copy-start.1 = (bf16[64,3072]{1,0:T(8,128)(2,1)S(1)}, bf16[64,3072]{1,0:T(8,128)(2,1)}, u32[]{:S(2)}) copy-start(bf16[64,3072]{1,0:T(8,128)(2,1)} %param.9) | copy-start | bytes 1179652
  37.5 198.0 %copy-start.2 = (f32[3072]{0:T(1024)S(1)}, f32[3072]{0:T(1024)}, u32[]{:S(2)}) copy-start(f32[3072]{0:T(1024)} %param.16) | copy-start | bytes 36868
  72.5 9.3 %all-to-all-start = ((bf16[2,64,1536]{2,1,0:T(8,128)(2,1)}), bf16[2,64,1536]{2,1,0:T(8,128)(2,1)S(1)}, u32[]{:S(2)}, u32[]{:S(2)}) async-start(bf16[2,64,1536]{2,1,0:T(8,128)(2,1)} %bitcast.4), calls=%async_computation | async-start | bytes 786432 | tf_op jit(solution)/shard_map/all_to_all | solution.py:35
  76.0 40.0 %all-reduce.4.cloned.1.call-start = ((), (), s32[]{:S(2)}) async-start(), calls=%async_computation.1 | async-start | bytes 1572864 | tf_op jit(solution)/shard_map/psum | solution.py:43
  83.3 152.1 %all-gather.2.cloned.1.call-start = ((), (), s32[]{:S(2)}) async-start(), calls=%async_computation.2 | async-start | bytes 18874368 | tf_op jit(solution)/shard_map/all_gather | solution.py:54
  117.3 125.2 %copy-start = (bf16[64,3072]{1,0:T(8,128)(2,1)}, bf16[64,3072]{1,0:T(8,128)(2,1)S(1)}, u32[]{:S(2)}) copy-start(bf16[64,3072]{1,0:T(8,128)(2,1)S(1)} %get-tuple-element.7) | copy-start | bytes 1179652
  235.5 40.3 %copy-start.5 = (s32[64]{0:T(128)S(1)}, s32[64]{0:T(128)}, u32[]{:S(2)}) copy-start(s32[64]{0:T(128)} %param.12) | copy-start | bytes 772
Sparse Core Ops, SparseCore 0:
  83.4 32.4 all-reduce.3
Sparse Core Ops, SparseCore 1:
  85.4 150.0 all-gather.1
where the time goes:
time: 314 us
  waiting for transfers between devices  156 us (50%)
  blocking collectives  119 us (38%)
  matrix products  15.9 us (5%)
  between operations  15.7 us (5%)
  starting transfers between devices  3.55 us (1%)
    all_gather x1, waiting for transfers between devices, per_device(): lax.all_gather(lens_head, 'dp', axis=0, tiled=True)  118 us
    psum x1, blocking collectives, per_device(): expert_out = lax.psum(partial_value, 'mp').astype(jnp.bfloat16)  35 us
    pmax x1, blocking collectives, per_device(): global_top = lax.pmax(local_top, ('expert', 'mp'))  33.2 us
    psum x1, waiting for transfers between devices, per_device(): summed = lax.psum(contrib, 'expert')  32 us
    psum x1, blocking collectives, per_device(): lax.psum((local_total, target_local), ('expert', 'mp'))  29.7 us
    all_gather x1, blocking collectives, per_device(): shard_part = lax.all_gather(picked, 'dp', axis=0, tiled=True)  12.7 us
    all_gather x1, blocking collectives, per_device(): lax.all_gather(hidden, 'dp', axis=1, tiled=True)  8.17 us
    dot_general x1, matrix products, per_device(): jnp.dot(normed, lax.all_gather(lens_head, 'dp', axis=0, tiled=True), pref...  7.05 us
  transfers between devices with their start and end apart: 3, of which 3 were waited for; matrix products, arithmetic and copies ran while one was open for 0% of the time, Pallas kernels for 0%

commit v1 on v0

v1 whole, which is shorter than its diff:
```python
import jax
import jax.numpy as jnp
from jax import lax
from jax.sharding import PartitionSpec as P

f32, bf16 = jnp.float32, jnp.bfloat16


def per_device(
    tokens, expert_ids, gate_values, targets, w_gate, w_up, w_down, norm_gain, lens_head
):
    rows, feats = tokens.shape
    owner = lax.axis_index("expert")
    weights = jnp.sum(jnp.where(expert_ids == owner, gate_values, f32(0.0)), axis=1)
    gate_mat = w_gate.reshape(feats, -1)
    up_mat = w_up.reshape(feats, -1)
    down_mat = w_down.reshape(w_down.shape[2], w_down.shape[3])
    own_feats = down_mat.shape[1]
    all_tokens = lax.all_gather(tokens, "dp", axis=0, tiled=True)
    all_weights = lax.all_gather(weights, "dp", axis=0, tiled=True)
    gate_part = jnp.dot(all_tokens, gate_mat, preferred_element_type=f32)
    up_part = jnp.dot(all_tokens, up_mat, preferred_element_type=f32)
    hidden = (jax.nn.silu(gate_part) * up_part).astype(bf16)
    hidden = lax.all_gather(hidden, "dp", axis=1, tiled=True)
    part = jnp.dot(hidden, down_mat, preferred_element_type=f32) * all_weights[:, None]
    summed = lax.psum(part, ("expert", "mp"))
    first = lax.axis_index("dp") * own_feats
    own_tokens = lax.dynamic_slice_in_dim(all_tokens, first, own_feats, axis=1)
    own_gain = lax.dynamic_slice_in_dim(norm_gain, first, own_feats, axis=0)
    mixed_part = (own_tokens.astype(f32) + summed).astype(bf16)
    mixed = lax.all_to_all(mixed_part, "dp", split_axis=0, concat_axis=1, tiled=True)
    mixed_f = mixed.astype(f32)
    scale = lax.rsqrt(jnp.mean(mixed_f * mixed_f, axis=1) + 1e-05)
    gained = (mixed_part.astype(f32) * own_gain[None, :]).astype(bf16)
    logits_part = jnp.dot(gained, lens_head, preferred_element_type=f32)
    logits = lax.psum_scatter(logits_part, "dp", scatter_dimension=0, tiled=True)
    logits = logits * scale[:, None]
    vocab_cols = lens_head.shape[1]
    vocab_start = (owner * lax.axis_size("mp") + lax.axis_index("mp")) * vocab_cols
    columns = vocab_start + lax.broadcasted_iota(jnp.int32, (1, vocab_cols), 1)
    hit = columns == targets[:, None]
    target_local = jnp.sum(jnp.where(hit, logits, f32(0.0)), axis=1)
    top = jnp.max(logits, axis=1)
    total = jnp.sum(jnp.exp(logits - top[:, None]), axis=1)
    stats = lax.all_gather(jnp.stack([top, total, target_local]), ("expert", "mp"))
    tops, totals, hits = stats[:, 0], stats[:, 1], stats[:, 2]
    top_all = jnp.max(tops, axis=0)
    exp_total = jnp.sum(totals * jnp.exp(tops - top_all[None, :]), axis=0)
    log_probs = jnp.sum(hits, axis=0) - top_all - jnp.log(exp_total)
    return (mixed, log_probs)


def solution(mesh):
    in_specs = (
        P("dp", None),
        P("dp", None),
        P("dp", None),
        P("dp"),
        P("expert", None, "mp", "dp"),
        P("expert", None, "mp", "dp"),
        P("expert", "mp", None, "dp"),
        P(),
        P("dp", ("expert", "mp")),
    )
    out_specs = (P("dp", None), P("dp"))
    return jax.shard_map(
        per_device, mesh=mesh, in_specs=in_specs, out_specs=out_specs, check_vma=False
    )
```

time: 314 us -> 208 us (0.66)
  blocking collectives: 119 us -> 56.8 us
  waiting for transfers between devices: 156 us -> 111 us
    all_gather x1 -> x0, waiting for transfers between devices: 118 us -> none  [per_device(): lax.all_gather(lens_head, 'dp', axis=0, tiled=True)]
    psum x2 -> x0, blocking collectives: 64.7 us -> none  [the longest x1 35 us: per_device(): expert_out = lax.psum(partial_value, 'mp').astype(jnp.bfloat16)]
    psum x1, waiting for transfers between devices: 32 us -> 93.2 us  [per_device(): summed = lax.psum(part, ('expert', 'mp'))]
    pmax x1 -> x0, blocking collectives: 33.2 us -> none  [per_device(): global_top = lax.pmax(local_top, ('expert', 'mp'))]
    all_gather x2 -> x3, blocking collectives: 20.9 us -> 51.8 us  [the longest x1 30.6 us: per_device(): lax.all_gather(jnp.stack([top, total, target_local]), ('expert', 'mp'))]
    reduce_scatter x0 -> x1, waiting for transfers between devices: none -> 7.19 us  [per_device(): lax.psum_scatter(logits_part, 'dp', scatter_dimension=0, tiled=True)]
    unnamed x0 -> x1, blocking collectives: none -> 4.92 us
    all_to_all x1, waiting for transfers between devices: 5.77 us -> 10.2 us  [per_device(): lax.all_to_all(mixed_part, 'dp', split_axis=0, concat_axis=1, tiled=True)]
  transfers between devices with their start and end apart: 3 -> 3, of which waited for: 3 -> 3; matrix products, arithmetic and copies ran while one was open for 0% -> 1% of each run, Pallas kernels for 0% -> 0%
where the time goes in v1:
time: 208 us; the launch traced here: 207 us
  waiting for transfers between devices  111 us (53%)
  blocking collectives  56.8 us (27%)
  between operations  14.9 us (7%)
  matrix products  14.6 us (7%)
  other arithmetic  5.39 us (3%)
  starting transfers between devices  3.56 us (2%)
    psum x1, waiting for transfers between devices, per_device(): summed = lax.psum(part, ('expert', 'mp'))  93.2 us
    all_gather x1, blocking collectives, per_device(): lax.all_gather(jnp.stack([top, total, target_local]), ('expert', 'mp'))  30.6 us
    all_gather x1, blocking collectives, per_device(): all_tokens = lax.all_gather(tokens, 'dp', axis=0, tiled=True)  13.1 us
    all_to_all x1, waiting for transfers between devices, per_device(): lax.all_to_all(mixed_part, 'dp', split_axis=0, concat_axis=1, tiled=True)  10.2 us
    all_gather x1, blocking collectives, per_device(): hidden = lax.all_gather(hidden, 'dp', axis=1, tiled=True)  8.17 us
    reduce_scatter x1, waiting for transfers between devices, per_device(): lax.psum_scatter(logits_part, 'dp', scatter_dimension=0, tiled=True)  7.19 us
    unnamed x1, blocking collectives  4.92 us
    dot_general x1, matrix products, per_device(): logits_part = jnp.dot(gained, lens_head, preferred_element_type=f32)  4.91 us
  transfers between devices with their start and end apart: 3, of which 3 were waited for; matrix products, arithmetic and copies ran while one was open for 1% of the time, Pallas kernels for 0%

profile of v1, /device:TPU:0, one launch (start us, length us, event | category | flops | bytes accessed | tf_op | source)
XLA Modules:
  0.0 207.5 jit_solution(1650163457520954662)
XLA Ops:
  7.2 0.0 all-reduce.3.cloned.1.call-start
  7.2 0.0 slice-start
  7.2 13.1 %all_gather.15 = bf16[128,3072]{1,0:T(8,128)(2,1)S(1)} all-gather(bf16[64,3072]{1,0:T(8,128)(2,1)} %param.9), channel_id=1, replica_groups=mesh['dp'=2,'expert'=4,'mp'=4] {'dp'}, dimensions={0}, use_global_device_ids=true | all-gather | bytes 1179648 | tf_op jit(solution)/shard_map/all_gather | solution.py:19
  20.3 3.9 %fusion.4 = f32[128,1024]{1,0:T(8,128)S(1)} fusion(bf16[128,3072]{1,0:T(8,128)(2,1)S(1)} %all_gather.15, bf16[1,3072,1,1024]{3,1,2,0:T(8,128)(2,1)} %param.13), kind=kOutput, calls=%fused_computation.4 | convolution fusion | flops 805306368 | bytes 7602176 | tf_op jit(solution)/shard_map/dot_general | solution.py:21
  24.2 0.0 slice-done
  24.2 0.0 slice-done.1
  24.3 0.0 copy-start.4
  24.3 0.0 copy-start.1
  24.3 0.0 copy-start.2
  24.3 1.1 fusion.12
  25.4 8.2 %all_gather.16 = bf16[128,2048]{1,0:T(8,128)(2,1)S(1)} all-gather(bf16[128,1024]{1,0:T(8,128)(2,1)S(1)} %fusion.12), channel_id=1, replica_groups=mesh['dp'=2,'expert'=4,'mp'=4] {'dp'}, dimensions={1}, use_global_device_ids=true | all-gather | bytes 786432 | tf_op jit(solution)/shard_map/all_gather | solution.py:24
  33.6 0.0 copy-done.4
  33.6 0.6 dynamic-slice
  34.9 0.2 dynamic-update-slice
  35.1 4.9 %all-reduce = f32[128]{0:T(128)S(1)} all-reduce(f32[128]{0:T(128)S(1)} %dynamic-update-slice), channel_id=1, replica_groups=mesh['dp'=2,'expert'=4,'mp'=4] {'dp'}, use_global_device_ids=true, to_apply=%add | all-reduce | flops 128 | bytes 1024
  40.0 4.7 %fusion.6 = f32[128,1536]{1,0:T(8,128)} fusion(bf16[128,2048]{1,0:T(8,128)(2,1)S(1)} %all_gather.16, bf16[1,1,2048,1536]{3,2,1,0:T(8,128)(2,1)} %param.15, f32[128]{0:T(128)S(1)} %all-reduce), kind=kOutput, calls=%fused_computation.6 | convolution fusion | flops 805502976 | bytes 7602688 | tf_op jit(solution)/shard_map/dot_general | solution.py:25
  44.7 0.0 all-reduce.3.cloned.1.call-update
  44.7 0.0 reduce-scatter.2.cloned.1.call-start
  44.8 0.1 dynamic_slice.7
  44.9 93.2 %all-reduce.3.cloned.1.call-done = f32[128,1536]{1,0:T(8,128)} async-done(((f32[128,1536]{1,0:T(8,128)}), f32[128,1536]{1,0:T(8,128)}) %all-reduce.3.cloned.1.call-update) | async-done | bytes 786448 | tf_op jit(solution)/shard_map/psum | solution.py:26
  138.1 1.9 add_convert_fusion
  140.0 4.9 %fusion.15 = f32[128,2048]{1,0:T(8,128)} fusion(bf16[1536,2048]{1,0:T(8,128)(2,1)} %param.17, bf16[128,1536]{1,0:T(8,128)(2,1)} %add_convert_fusion, f32[1536]{0:T(1024)S(1)} %dynamic_slice.7), kind=kOutput, calls=%fused_computation.15 | convolution fusion | flops 805896192 | bytes 7739392 | tf_op jit(solution)/shard_map/dot_general | solution.py:35
  144.9 0.0 reduce-scatter.2.cloned.1.call-update
  145.0 3.5 %all-to-all-start = ((bf16[2,64,1536]{2,1,0:T(8,128)(2,1)}), bf16[2,64,1536]{2,1,0:T(8,128)(2,1)S(1)}, u32[]{:S(2)}, u32[]{:S(2)}) async-start(bf16[2,64,1536]{2,1,0:T(8,128)(2,1)} %bitcast.4), calls=%async_computation | async-start | bytes 786432 | tf_op jit(solution)/shard_map/all_to_all | solution.py:31
  148.5 10.2 %all-to-all-done = bf16[2,64,1536]{2,1,0:T(8,128)(2,1)S(1)} async-done(((bf16[2,64,1536]{2,1,0:T(8,128)(2,1)}), bf16[2,64,1536]{2,1,0:T(8,128)(2,1)S(1)}, u32[]{:S(2)}, u32[]{:S(2)}) %all-to-all-start) | async-done | bytes 393248 | tf_op jit(solution)/shard_map/all_to_all | solution.py:31
  158.6 0.8 copy.16
  159.4 0.2 multiply_reduce_fusion
  159.6 7.2 %reduce-scatter.2.cloned.1.call-done = f32[64,2048]{1,0:T(8,128)} async-done(((f32[128,2048]{1,0:T(8,128)}), f32[64,2048]{1,0:T(8,128)}) %reduce-scatter.2.cloned.1.call-update) | async-done | bytes 524304 | tf_op jit(solution)/shard_map/reduce_scatter | solution.py:36
  166.8 1.2 multiply_reduce_fusion.1
  168.0 1.4 exponential_reduce_fusion
  169.4 30.6 %all-gather.1 = f32[16,3,64]{2,1,0:T(4,128)S(1)} all-gather(f32[1,3,64]{2,1,0:T(4,128)S(1)} %maximum_bitcast_fusion), channel_id=2, replica_groups=mesh['dp'=2,'expert'=4,'mp'=4] {'expert','mp'}, dimensions={0}, use_global_device_ids=true | all-gather | bytes 13056 | tf_op jit(solution)/shard_map/all_gather | solution.py:45
  200.1 0.5 log_subtract_fusion
  (15 shorter events, 0.1 us)
Async XLA Ops:
  7.2 130.9 %all-reduce.3.cloned.1.call-start = ((), (), s32[]{:S(2)}) async-start(), calls=%async_computation.2 | async-start | bytes 1572864 | tf_op jit(solution)/shard_map/psum | solution.py:26
  7.2 17.0 %slice-start = ((s8[6291456]{0:T(1024)(128)(4,1)}), s8[4194304]{0:T(1024)(128)(4,1)S(1)}, s32[]{:S(2)}) async-start(s8[6291456]{0:T(1024)(128)(4,1)} %bitcast.41), calls=%async_computation.4 | async-start | bytes 8388608
  20.3 3.9 %slice-start.1 = ((s8[6291456]{0:T(1024)(128)(4,1)}), s8[2097152]{0:T(1024)(128)(4,1)S(1)}, s32[]{:S(2)}) async-start(s8[6291456]{0:T(1024)(128)(4,1)} %bitcast.41), calls=%async_computation.5 | async-start | bytes 4194304
  24.3 9.3 %copy-start.4 = (u32[32]{0:T(128)S(1)}, u32[32]{0:T(128)}, u32[]{:S(2)}) copy-start(u32[32]{0:T(128)} %constant.40) | copy-start | bytes 388
  24.3 10.5 %copy-start.1 = (f32[64,2]{0,1:T(2,128)S(1)}, f32[64,2]{0,1:T(2,128)}, u32[]{:S(2)}) copy-start(f32[64,2]{0,1:T(2,128)} %param.11) | copy-start | bytes 1540
  24.3 10.5 %copy-start.2 = (s32[64,2]{0,1:T(2,128)S(1)}, s32[64,2]{0,1:T(2,128)}, u32[]{:S(2)}) copy-start(s32[64,2]{0,1:T(2,128)} %param.10) | copy-start | bytes 1540
  40.0 4.8 %copy-start = (f32[3072]{0:T(1024)S(1)}, f32[3072]{0:T(1024)}, u32[]{:S(2)}) copy-start(f32[3072]{0:T(1024)} %param.16) | copy-start | bytes 36868
  44.7 122.0 %reduce-scatter.2.cloned.1.call-start = ((), (), s32[]{:S(2)}) async-start(), calls=%async_computation.3 | async-start | bytes 1572864 | tf_op jit(solution)/shard_map/reduce_scatter | solution.py:36
  44.9 123.1 %copy-start.3 = (s32[64]{0:T(128)S(1)}, s32[64]{0:T(128)}, u32[]{:S(2)}) copy-start(s32[64]{0:T(128)} %param.12) | copy-start | bytes 772
  145.0 13.7 %all-to-all-start = ((bf16[2,64,1536]{2,1,0:T(8,128)(2,1)}), bf16[2,64,1536]{2,1,0:T(8,128)(2,1)S(1)}, u32[]{:S(2)}, u32[]{:S(2)}) async-start(bf16[2,64,1536]{2,1,0:T(8,128)(2,1)} %bitcast.4), calls=%async_computation | async-start | bytes 786432 | tf_op jit(solution)/shard_map/all_to_all | solution.py:31
Sparse Core Ops, SparseCore 0:
  44.9 93.1 all-reduce.2
  145.1 21.6 reduce-scatter.1

commit v2 on v1

--- a/solution.py
+++ b/solution.py
@@ -1,6 +1,8 @@
 import jax
 import jax.numpy as jnp
 from jax import lax
+from jax.experimental import pallas as pl
+from jax.experimental.pallas import tpu as pltpu
 from jax.sharding import PartitionSpec as P
 
 f32, bf16 = jnp.float32, jnp.bfloat16
@@ -50,6 +52,367 @@
     return (mixed, log_probs)
 
 
+HC = 256
+LC = 512
+
+
+def fused_kernel(
+    tok_hbm, w_own, targets, wg_hbm, wu_hbm, wd_hbm, gain, lens_hbm,
+    mixed_out, lp_out,
+    tok, wts, wg, wu, wd, lens, h, acc, core_tx, core_rx, rs_tx, rs_rx, mix, xmix,
+    gained, own_lg, lg_tx, lg_rx, stats,
+    ld_sem, wg_sem, wu_sem, tok_s, tok_r, h_s, h_r, core_s, core_r,
+    rs_s, rs_r, ag_s, ag_r, fw_s, fw_r, xm_s, xm_r, lg_s, lg_r, st_s, st_r,
+):
+    slab, feats = tok_hbm.shape
+    hid = wg_hbm.shape[1]
+    half = wd_hbm.shape[1]
+    quarter = half // 2
+    vocab = lens_hbm.shape[1]
+    n_hc, n_lc = hid // HC, vocab // LC
+    x, e, m = lax.axis_index("dp"), lax.axis_index("expert"), lax.axis_index("mp")
+    n_mp = lax.axis_size("mp")
+    n_plane = lax.axis_size("expert") * n_mp
+    n_chip = n_plane // 2
+    c = e % 2
+    y = e // 2
+    q = y * n_mp + m
+    p = e * n_mp + m
+    rb = 2 * slab // n_chip
+    xp = 1 - x
+    xdev = {"dp": xp}
+    cdev = {"expert": y * 2 + 1 - c}
+
+    def chip(d):
+        t = (q + d) % n_chip
+        return {"expert": (t // n_mp) * 2 + c, "mp": t % n_mp}
+
+    def plane(d):
+        t = (p + d) % n_plane
+        return {"expert": t // n_mp, "mp": t % n_mp}
+
+    def rcopy(src, dst, ss, rs, dev):
+        return pltpu.make_async_remote_copy(
+            src_ref=src, dst_ref=dst, send_sem=ss, recv_sem=rs,
+            device_id=dev, device_id_type=pl.DeviceIdType.MESH,
+        )
+
+    def rows(who):
+        return pl.ds(pl.multiple_of(who * slab, slab), slab)
+
+    def lanes(start, size):
+        return pl.ds(pl.multiple_of(start, 128), size)
+
+    own_tok = pltpu.make_async_copy(tok_hbm, tok.at[rows(x)], ld_sem.at[0])
+    own_tok.start()
+
+    def wload(j):
+        cols = lanes(j * HC, HC)
+        return (
+            pltpu.make_async_copy(wg_hbm.at[:, cols], wg.at[:, cols], wg_sem.at[j]),
+            pltpu.make_async_copy(wu_hbm.at[:, cols], wu.at[:, cols], wu_sem.at[j]),
+        )
+
+    for j in range(n_hc):
+        for copy in wload(j):
+            copy.start()
+    down_load = pltpu.make_async_copy(wd_hbm, wd, ld_sem.at[1])
+    down_load.start()
+    lens_load = pltpu.make_async_copy(lens_hbm, lens, ld_sem.at[2])
+    lens_load.start()
+
+    barrier = pltpu.get_barrier_semaphore()
+    pl.semaphore_signal(barrier, inc=1, device_id=xdev, device_id_type=pl.DeviceIdType.MESH)
+    for d in range(1, n_plane):
+        pl.semaphore_signal(
+            barrier, inc=1, device_id=plane(d), device_id_type=pl.DeviceIdType.MESH
+        )
+    own_tok.wait()
+    pl.semaphore_wait(barrier, n_plane)
+
+    sends = []
+    part = slab // 2
+    mine = tok.at[pl.ds(pl.multiple_of(x * slab + c * part, part), part)]
+    tok_x = rcopy(mine, mine, tok_s.at[0], tok_r.at[0], xdev)
+    tok_x.start()
+    wts[rows(x), :] = w_own[...]
+    w_x = rcopy(wts.at[rows(x)], wts.at[rows(x)], tok_s.at[2], tok_r.at[2], xdev)
+    w_x.start()
+
+    def hcopy(k, j):
+        who = x if k == 0 else xp
+        block = h.at[rows(who), lanes(x * hid + j * HC, HC)]
+        return rcopy(block, block, h_s.at[k * n_hc + j], h_r.at[k * n_hc + j], xdev)
+
+    def hidden_steps(k):
+        who = x if k == 0 else xp
+
+        def step(j, carry):
+            if k == 0:
+                for copy in wload(j):
+                    copy.wait()
+            t = tok[rows(who), :]
+            cols = lanes(j * HC, HC)
+            g = jnp.dot(t, wg[:, cols], preferred_element_type=f32)
+            u = jnp.dot(t, wu[:, cols], preferred_element_type=f32)
+            h[rows(who), lanes(x * hid + j * HC, HC)] = (jax.nn.silu(g) * u).astype(bf16)
+            hcopy(k, j).start()
+            return carry
+
+        lax.fori_loop(0, n_hc, step, 0)
+
+    tok_x.wait_recv()
+    theirs = tok.at[pl.ds(pl.multiple_of(xp * slab + c * part, part), part)]
+    tok_c = rcopy(theirs, theirs, tok_s.at[1], tok_r.at[1], cdev)
+    tok_c.start()
+    hidden_steps(0)
+    tok_c.wait_recv()
+    hidden_steps(1)
+
+    down_load.wait()
+    n_dc = half // HC
+
+    def down_own(j, carry):
+        cols = lanes(j * HC, HC)
+        acc[:, cols] = jnp.dot(
+            h[:, lanes(x * hid, hid)],
+            wd[pl.ds(pl.multiple_of(x * hid, hid), hid), cols],
+            preferred_element_type=f32,
+        )
+        return carry
+
+    lax.fori_loop(0, n_dc, down_own, 0)
+    w_x.wait_recv()
+
+    def hwait(j, carry):
+        hcopy(0, j).wait_recv()
+        hcopy(1, j).wait_recv()
+        return carry
+
+    lax.fori_loop(0, n_hc, hwait, 0)
+
+    def down_other(j, first):
+        cols = lanes(first + j * HC, HC)
+        more = jnp.dot(
+            h[:, lanes(xp * hid, hid)],
+            wd[pl.ds(pl.multiple_of(xp * hid, hid), hid), cols],
+            preferred_element_type=f32,
+        )
+        return (acc[:, cols] + more) * wts[:, 0:1]
+
+    def down_give(j, carry):
+        core_tx[:, lanes(j * HC, HC)] = down_other(j, (1 - c) * quarter)
+        return carry
+
+    lax.fori_loop(0, n_dc // 2, down_give, 0)
+    core_x = rcopy(core_tx, core_rx, core_s, core_r, cdev)
+    core_x.start()
+
+    def down_keep(j, carry):
+        value = down_other(j, c * quarter)
+        acc[:, lanes(c * quarter + j * HC, HC)] = value
+        return carry
+
+    lax.fori_loop(0, n_dc // 2, down_keep, 0)
+    core_x.wait_recv()
+    kept = lanes(c * quarter, quarter)
+    core_rx[...] = core_rx[...] + acc[:, kept]
+    rs_tx[...] = core_rx[...].astype(bf16)
+
+    def blk(who):
+        return pl.ds(pl.multiple_of(who * rb, rb), rb)
+
+    rs = []
+    for d in range(1, n_chip):
+        copy = rcopy(
+            rs_tx.at[blk((q + d) % n_chip)], rs_rx.at[d - 1], rs_s.at[d - 1], rs_r.at[d - 1], chip(d)
+        )
+        copy.start()
+        rs.append(copy)
+    total = core_rx[blk(q), :]
+    total = total + tok[blk(q), lanes(x * half + c * quarter, quarter)].astype(f32)
+    for d in range(1, n_chip):
+        rs[d - 1].wait_recv()
+        total = total + rs_rx[d - 1].astype(f32)
+    mix[blk(q), kept] = total.astype(bf16)
+
+    ag = []
+    block = mix.at[blk(q), kept]
+    for d in range(1, n_chip):
+        copy = rcopy(block, block, ag_s.at[d - 1], ag_r.at[d - 1], chip(d))
+        copy.start()
+        ag.append(copy)
+    fw = [rcopy(block, block, fw_s.at[0], fw_r.at[0], cdev)]
+    fw[0].start()
+    for d in range(1, n_chip):
+        ag[d - 1].wait_recv()
+        got = mix.at[blk((q + n_chip - d) % n_chip), kept]
+        copy = rcopy(got, got, fw_s.at[d], fw_r.at[d], cdev)
+        copy.start()
+        fw.append(copy)
+    xm = rcopy(mix.at[rows(xp), kept], xmix.at[:, kept], xm_s.at[0], xm_r.at[0], xdev)
+    xm.start()
+    for copy in fw:
+        copy.wait_recv()
+    gained[...] = (mix[...].astype(f32) * gain[:, lanes(x * half, half)]).astype(bf16)
+    lens_load.wait()
+
+    def lgcopy(j):
+        cols = lanes(j * LC, LC)
+        return rcopy(lg_tx.at[:, cols], lg_rx.at[:, cols], lg_s.at[j], lg_r.at[j], xdev)
+
+    def logits_give(j, carry):
+        cols = lanes(j * LC, LC)
+        lg_tx[:, cols] = jnp.dot(
+            gained[rows(xp), :], lens[:, cols], preferred_element_type=f32
+        ).astype(bf16)
+        lgcopy(j).start()
+        return carry
+
+    lax.fori_loop(0, n_lc, logits_give, 0)
+
+    xm.wait_recv()
+    xf = rcopy(xmix.at[:, kept], xmix.at[:, kept], xm_s.at[1], xm_r.at[1], cdev)
+    xf.start()
+
+    def logits_keep(j, carry):
+        cols = lanes(j * LC, LC)
+        own_lg[:, cols] = jnp.dot(
+            gained[rows(x), :], lens[:, cols], preferred_element_type=f32
+        )
+        return carry
+
+    lax.fori_loop(0, n_lc, logits_keep, 0)
+
+    mine_mix = mix[rows(x), :]
+    mixed_out[:, lanes(x * half, half)] = mine_mix
+    xf.wait_recv()
+    other_mix = xmix[...]
+    mixed_out[:, lanes(xp * half, half)] = other_mix
+    a, b = mine_mix.astype(f32), other_mix.astype(f32)
+    square = jnp.sum(a * a, axis=1, keepdims=True) + jnp.sum(b * b, axis=1, keepdims=True)
+    scale = lax.rsqrt(square / feats + 1e-05)
+
+    top = jnp.full((slab, 1), -jnp.inf, f32)
+    hit = jnp.zeros((slab, 1), f32)
+    for j in range(n_lc):
+        cols = pl.ds(j * LC, LC)
+        lgcopy(j).wait_recv()
+        value = (own_lg[:, cols] + lg_rx[:, cols].astype(f32)) * scale
+        own_lg[:, cols] = value
+        top = jnp.maximum(top, jnp.max(value, axis=1, keepdims=True))
+        place = p * vocab + j * LC + lax.broadcasted_iota(jnp.int32, (slab, LC), 1)
+        hit = hit + jnp.sum(
+            jnp.where(place == targets[...], value, f32(0.0)), axis=1, keepdims=True
+        )
+    summed = jnp.zeros((slab, 1), f32)
+    for j in range(n_lc):
+        summed = summed + jnp.sum(
+            jnp.exp(own_lg[:, pl.ds(j * LC, LC)] - top), axis=1, keepdims=True
+        )
+    lane = lax.broadcasted_iota(jnp.int32, (slab, 128), 1)
+    packed = jnp.where(lane == 0, top, jnp.where(lane == 1, summed, hit))
+    packed = jnp.concatenate([packed, packed], axis=0)
+    stats[0] = packed.T[0:8, :]
+    st = []
+    for d in range(1, n_plane):
+        copy = rcopy(stats.at[0], stats.at[d], st_s.at[d - 1], st_r.at[d - 1], plane(d))
+        copy.start()
+        st.append(copy)
+    for copy in st:
+        copy.wait_recv()
+    every = stats[...]
+    tops, sums, hits = every[:, 0:1, :], every[:, 1:2, :], every[:, 2:3, :]
+    top_all = jnp.max(tops, axis=0)
+    exp_total = jnp.sum(sums * jnp.exp(tops - top_all[None]), axis=0)
+    result = jnp.sum(hits, axis=0) - top_all - jnp.log(exp_total)
+    lp_out[...] = jnp.broadcast_to(result, lp_out.shape)
+
+    for copy in [tok_x, w_x, tok_c, core_x, xm, xf] + rs + ag + fw + st:
+        copy.wait_send()
+
+    def hdone(j, carry):
+        hcopy(0, j).wait_send()
+        hcopy(1, j).wait_send()
+        return carry
+
+    lax.fori_loop(0, n_hc, hdone, 0)
+
+    def lgdone(j, carry):
+        lgcopy(j).wait_send()
+        return carry
+
+    lax.fori_loop(0, n_lc, lgdone, 0)
+
+
+def per_device_fused(
+    tokens, expert_ids, gate_values, targets, w_gate, w_up, w_down, norm_gain, lens_head
+):
+    slab, feats = tokens.shape
+    owner = lax.axis_index("expert")
+    weights = jnp.sum(jnp.where(expert_ids == owner, gate_values, f32(0.0)), axis=1)
+    weights = jnp.broadcast_to(weights[:, None], (slab, 128))
+    wg = w_gate.reshape(feats, -1)
+    wu = w_up.reshape(feats, -1)
+    wd = w_down.reshape(w_down.shape[2], w_down.shape[3])
+    hid, half, vocab = wg.shape[1], wd.shape[1], lens_head.shape[1]
+    n_plane = lax.axis_size("expert") * lax.axis_size("mp")
+    n_chip = n_plane // 2
+    all_rows = 2 * slab
+    n_hc, n_lc = hid // HC, vocab // LC
+    dma = pltpu.SemaphoreType.DMA
+    vmem = pl.BlockSpec(memory_space=pltpu.VMEM)
+    hbm = pl.BlockSpec(memory_space=pl.ANY)
+    flops = 2 * all_rows * (2 * feats * hid + 2 * hid * half + half * vocab)
+    mixed, lp = pl.pallas_call(
+        fused_kernel,
+        out_shape=(
+            jax.ShapeDtypeStruct((slab, feats), bf16),
+            jax.ShapeDtypeStruct((8, 128), f32),
+        ),
+        in_specs=[hbm, vmem, vmem, hbm, hbm, hbm, vmem, hbm],
+        out_specs=(vmem, vmem),
+        scratch_shapes=[
+            pltpu.VMEM((all_rows, feats), bf16),
+            pltpu.VMEM((all_rows, 128), f32),
+            pltpu.VMEM(wg.shape, bf16),
+            pltpu.VMEM(wu.shape, bf16),
+            pltpu.VMEM(wd.shape, bf16),
+            pltpu.VMEM(lens_head.shape, bf16),
+            pltpu.VMEM((all_rows, 2 * hid), bf16),
+            pltpu.VMEM((all_rows, half), f32),
+            pltpu.VMEM((all_rows, half // 2), f32),
+            pltpu.VMEM((all_rows, half // 2), f32),
+            pltpu.VMEM((all_rows, half // 2), bf16),
+            pltpu.VMEM((n_chip - 1, all_rows // n_chip, half // 2), bf16),
+            pltpu.VMEM((all_rows, half), bf16),
+            pltpu.VMEM((slab, half), bf16),
+            pltpu.VMEM((all_rows, half), bf16),
+            pltpu.VMEM((slab, vocab), f32),
+            pltpu.VMEM((slab, vocab), bf16),
+            pltpu.VMEM((slab, vocab), bf16),
+            pltpu.VMEM((n_plane, 8, 128), f32),
+            dma((3,)), dma((n_hc,)), dma((n_hc,)),
+            dma((3,)), dma((3,)),
+            dma((2 * n_hc,)), dma((2 * n_hc,)),
+            dma, dma,
+            dma((n_chip - 1,)), dma((n_chip - 1,)),
+            dma((n_chip - 1,)), dma((n_chip - 1,)),
+            dma((n_chip,)), dma((n_chip,)),
+            dma((2,)), dma((2,)),
+            dma((n_lc,)), dma((n_lc,)),
+            dma((n_plane - 1,)), dma((n_plane - 1,)),
+        ],
+        compiler_params=pltpu.CompilerParams(
+            collective_id=0, has_side_effects=True, vmem_limit_bytes=48 * 1024 * 1024
+        ),
+        cost_estimate=pl.CostEstimate(
+            flops=flops, bytes_accessed=4 * wg.size * 2, transcendentals=0
+        ),
+    )(tokens, weights, targets[:, None], wg, wu, wd, norm_gain[None, :], lens_head)
+    return (mixed, lp[0, :slab])
+
+
 def solution(mesh):
     in_specs = (
         P("dp", None),
@@ -63,6 +426,7 @@
         P("dp", ("expert", "mp")),
     )
     out_specs = (P("dp", None), P("dp"))
+    fused = mesh.shape["dp"] == 2 and mesh.shape["expert"] == 4 and mesh.shape["mp"] == 4
     return jax.shard_map(
-        per_device, mesh=mesh, in_specs=in_specs, out_specs=out_specs, check_vma=False
+        per_device_fused if fused else per_device, mesh=mesh, in_specs=in_specs, out_specs=out_specs, check_vma=False
     )

time: 208 us -> 56.5 us (0.27)
  waiting for transfers between devices: 111 us -> 0 us
  blocking collectives: 56.8 us -> 0 us
  Pallas kernels: 0 us -> 51.1 us
  matrix products: 14.6 us -> 0 us
  between operations: 14.9 us -> 0.65 us
  other arithmetic: 5.39 us -> 0.71 us
  starting transfers between devices: 3.56 us -> 0 us
    psum x1 -> x0, waiting for transfers between devices: 93.2 us -> none  [per_device(): summed = lax.psum(part, ('expert', 'mp'))]
    all_gather x3 -> x0, blocking collectives: 51.8 us -> none  [the longest x1 30.6 us: per_device(): lax.all_gather(jnp.stack([top, total, target_local]), ('expert', 'mp'))]
    pallas_call x0 -> x1, Pallas kernels: none -> 51.1 us  [per_device_fused(): pl.pallas_call(fused_kernel, out_shape=(jax.ShapeDtypeStruct((slab, feats...]
    dot_general x4 -> x0, matrix products: 14.6 us -> none  [the longest x1 4.91 us: per_device(): logits_part = jnp.dot(gained, lens_head, preferred_element_type=f32)]
    all_to_all x1 -> x0, waiting for transfers between devices: 10.2 us -> none  [per_device(): lax.all_to_all(mixed_part, 'dp', split_axis=0, concat_axis=1, tiled=True)]
    reduce_scatter x1 -> x0, waiting for transfers between devices: 7.19 us -> none  [per_device(): lax.psum_scatter(logits_part, 'dp', scatter_dimension=0, tiled=True)]
    unnamed x1 -> x0, blocking collectives: 4.92 us -> none
    all_to_all x1 -> x0, starting transfers between devices: 3.48 us -> none  [per_device(): lax.all_to_all(mixed_part, 'dp', split_axis=0, concat_axis=1, tiled=True)]
  transfers between devices with their start and end apart: 3 -> 0, of which waited for: 3 -> 0; matrix products, arithmetic and copies ran while one was open for 1% -> 0% of each run, Pallas kernels for 0% -> 0%
where the time goes in v2:
time: 56.5 us; the launch traced here: 56.3 us
  Pallas kernels  51.1 us (90%)
  local copies, waits for them, and re-layouts  3.78 us (7%)
  other arithmetic  0.71 us (1%)
  between operations  0.65 us (1%)
    pallas_call x1, Pallas kernels, per_device_fused(): pl.pallas_call(fused_kernel, out_shape=(jax.ShapeDtypeStruct((slab, feats...  51.1 us
    unnamed x5, local copies, waits for them, and re-layouts  2.45 us

profile of v2, /device:TPU:0, one launch (start us, length us, event | category | flops | bytes accessed | tf_op | source)
XLA Modules:
  0.0 56.3 jit_solution(117893796416944504)
XLA Ops:
  0.6 0.7 %fusion = f32[64]{0:T(128)S(1)} fusion(f32[64,2]{0,1:T(2,128)} %param.11, s32[64,2]{0,1:T(2,128)} %param.10, s32[]{:T(128)S(6)} %axis_index.15), kind=kLoop, calls=%fused_computation.1 | loop fusion | flops 320 | bytes 1284 | tf_op jit(solution)/shard_map/reduce_sum | solution.py:353
  1.3 0.1 broadcast_in_dim.17.w_own
  1.4 0.7 %copy.11.targets = s32[64,1]{1,0:T(8,128)S(1)} copy(s32[64,1]{0,1:T(1,128)} %bitcast.11) | data formatting | bytes 512 | tf_op jit(solution)/shard_map/broadcast_in_dim | solution.py:412
  2.2 0.0 copy-start
  2.2 1.0 %copy-done = bf16[64,3072]{1,0:T(8,128)(2,1)S(1)} copy-done((bf16[64,3072]{1,0:T(8,128)(2,1)S(1)}, bf16[64,3072]{1,0:T(8,128)(2,1)}, u32[]{:S(2)}) %copy-start) | copy-done | bytes 393240
  3.2 0.0 copy-start.1
  3.2 0.7 %copy-done.1 = f32[3072]{0:T(1024)S(1)} copy-done((f32[3072]{0:T(1024)S(1)}, f32[3072]{0:T(1024)}, u32[]{:S(2)}) %copy-start.1) | copy-done | bytes 12312
  3.9 51.1 %shard_map.104 = (bf16[64,3072]{1,0:T(8,128)(2,1)S(1)}, f32[8,128]{1,0:T(8,128)S(1)}) custom-call(bf16[64,3072]{1,0:T(8,128)(2,1)S(1)} %copy-done, f32[64,128]{1,0:T(8,128)S(1)} %broadcast_in_dim.17.w_own, s32[64,1]{1,0:T(8,128)S(1)} %copy.11.targets, bf16[3072,1024]{1,0:T(8,128)(2,1)} %bitcast.8, bf16[3072,1024]{1,0:T(8,128)(2,1)} %bitcast.9, ...), custom_call_target="tpu_custom_call" | custom-call | flops 3221225472 | bytes 25165824 | tf_op jit(solution)/shard_map/pallas_call | solution.py:367
  55.0 0.5 slice_bitcast_fusion
  55.5 0.7 %copy.13 = bf16[64,3072]{1,0:T(8,128)(2,1)} copy(bf16[64,3072]{1,0:T(8,128)(2,1)S(1)} %get-tuple-element.8) | data formatting | bytes 786432
Async XLA Ops:
  2.2 1.0 %copy-start = (bf16[64,3072]{1,0:T(8,128)(2,1)S(1)}, bf16[64,3072]{1,0:T(8,128)(2,1)}, u32[]{:S(2)}) copy-start(bf16[64,3072]{1,0:T(8,128)(2,1)} %tok_hbm.1) | copy-start | bytes 1179652
  3.2 0.7 %copy-start.1 = (f32[3072]{0:T(1024)S(1)}, f32[3072]{0:T(1024)}, u32[]{:S(2)}) copy-start(f32[3072]{0:T(1024)} %param.16) | copy-start | bytes 36868

commit v3 on v2

--- a/solution.py
+++ b/solution.py
@@ -57,10 +57,10 @@
 
 
 def fused_kernel(
-    tok_hbm, w_own, targets, wg_hbm, wu_hbm, wd_hbm, gain, lens_hbm,
+    tok_hbm, ids_hbm, gates_hbm, targets_hbm, wg_hbm, wu_hbm, wd_hbm, gain_hbm, lens_hbm,
     mixed_out, lp_out,
     tok, wts, wg, wu, wd, lens, h, acc, core_tx, core_rx, rs_tx, rs_rx, mix, xmix,
-    gained, own_lg, lg_tx, lg_rx, stats,
+    gained, own_lg, lg_tx, lg_rx, stats, ids, gates, targets, gain,
     ld_sem, wg_sem, wu_sem, tok_s, tok_r, h_s, h_r, core_s, core_r,
     rs_s, rs_r, ag_s, ag_r, fw_s, fw_r, xm_s, xm_r, lg_s, lg_r, st_s, st_r,
 ):
@@ -105,6 +105,14 @@
 
     own_tok = pltpu.make_async_copy(tok_hbm, tok.at[rows(x)], ld_sem.at[0])
     own_tok.start()
+    small = [
+        pltpu.make_async_copy(ids_hbm, ids, ld_sem.at[3]),
+        pltpu.make_async_copy(gates_hbm, gates, ld_sem.at[4]),
+        pltpu.make_async_copy(targets_hbm, targets, ld_sem.at[5]),
+        pltpu.make_async_copy(gain_hbm, gain, ld_sem.at[6]),
+    ]
+    for copy in small:
+        copy.start()
 
     def wload(j):
         cols = lanes(j * HC, HC)
@@ -135,7 +143,19 @@
     mine = tok.at[pl.ds(pl.multiple_of(x * slab + c * part, part), part)]
     tok_x = rcopy(mine, mine, tok_s.at[0], tok_r.at[0], xdev)
     tok_x.start()
-    wts[rows(x), :] = w_own[...]
+    for copy in small:
+        copy.wait()
+    w_row = jnp.sum(jnp.where(ids[...] == e, gates[...], f32(0.0)), axis=0, keepdims=True)
+    eye = lax.broadcasted_iota(jnp.int32, (slab, slab), 0) == lax.broadcasted_iota(
+        jnp.int32, (slab, slab), 1
+    )
+
+    def column(row, zero):
+        return jnp.sum(
+            jnp.where(eye, jnp.broadcast_to(row, (slab, slab)), zero), axis=1, keepdims=True
+        )
+
+    wts[rows(x), :] = jnp.broadcast_to(column(w_row, f32(0.0)), (slab, 128))
     w_x = rcopy(wts.at[rows(x)], wts.at[rows(x)], tok_s.at[2], tok_r.at[2], xdev)
     w_x.start()
 
@@ -144,7 +164,7 @@
         block = h.at[rows(who), lanes(x * hid + j * HC, HC)]
         return rcopy(block, block, h_s.at[k * n_hc + j], h_r.at[k * n_hc + j], xdev)
 
-    def hidden_steps(k):
+    def hidden_steps(k, first, last):
         who = x if k == 0 else xp
 
         def step(j, carry):
@@ -159,15 +179,16 @@
             hcopy(k, j).start()
             return carry
 
-        lax.fori_loop(0, n_hc, step, 0)
-
+        lax.fori_loop(first, last, step, 0)
+
+    hidden_steps(0, 0, n_hc // 2)
     tok_x.wait_recv()
     theirs = tok.at[pl.ds(pl.multiple_of(xp * slab + c * part, part), part)]
     tok_c = rcopy(theirs, theirs, tok_s.at[1], tok_r.at[1], cdev)
     tok_c.start()
-    hidden_steps(0)
+    hidden_steps(0, n_hc // 2, n_hc)
     tok_c.wait_recv()
-    hidden_steps(1)
+    hidden_steps(1, 0, n_hc)
 
     down_load.wait()
     n_dc = half // HC
@@ -200,39 +221,48 @@
         )
         return (acc[:, cols] + more) * wts[:, 0:1]
 
+    def core_x(j):
+        cols = lanes(j * HC, HC)
+        return rcopy(core_tx.at[:, cols], core_rx.at[:, cols], core_s.at[j], core_r.at[j], cdev)
+
     def down_give(j, carry):
         core_tx[:, lanes(j * HC, HC)] = down_other(j, (1 - c) * quarter)
+        core_x(j).start()
         return carry
 
     lax.fori_loop(0, n_dc // 2, down_give, 0)
-    core_x = rcopy(core_tx, core_rx, core_s, core_r, cdev)
-    core_x.start()
-
-    def down_keep(j, carry):
-        value = down_other(j, c * quarter)
-        acc[:, lanes(c * quarter + j * HC, HC)] = value
-        return carry
-
-    lax.fori_loop(0, n_dc // 2, down_keep, 0)
-    core_x.wait_recv()
-    kept = lanes(c * quarter, quarter)
-    core_rx[...] = core_rx[...] + acc[:, kept]
-    rs_tx[...] = core_rx[...].astype(bf16)
 
     def blk(who):
         return pl.ds(pl.multiple_of(who * rb, rb), rb)
 
-    rs = []
-    for d in range(1, n_chip):
-        copy = rcopy(
-            rs_tx.at[blk((q + d) % n_chip)], rs_rx.at[d - 1], rs_s.at[d - 1], rs_r.at[d - 1], chip(d)
-        )
-        copy.start()
-        rs.append(copy)
+    kept = lanes(c * quarter, quarter)
+    n_q = n_dc // 2
+
+    def rs_copy(j, d):
+        cols = lanes(j * HC, HC)
+        spot = (d - 1) * n_q + j
+        return rcopy(
+            rs_tx.at[blk((q + d) % n_chip), cols], rs_rx.at[d - 1, :, cols],
+            rs_s.at[spot], rs_r.at[spot], chip(d),
+        )
+
+    def down_keep(j, carry):
+        cols = lanes(j * HC, HC)
+        value = down_other(j, c * quarter)
+        core_x(j).wait_recv()
+        value = value + core_rx[:, cols]
+        core_rx[:, cols] = value
+        rs_tx[:, cols] = value.astype(bf16)
+        for d in range(1, n_chip):
+            rs_copy(j, d).start()
+        return carry
+
+    lax.fori_loop(0, n_q, down_keep, 0)
     total = core_rx[blk(q), :]
     total = total + tok[blk(q), lanes(x * half + c * quarter, quarter)].astype(f32)
     for d in range(1, n_chip):
-        rs[d - 1].wait_recv()
+        for j in range(n_q):
+            rs_copy(j, d).wait_recv()
         total = total + rs_rx[d - 1].astype(f32)
     mix[blk(q), kept] = total.astype(bf16)
 
@@ -293,6 +323,7 @@
     square = jnp.sum(a * a, axis=1, keepdims=True) + jnp.sum(b * b, axis=1, keepdims=True)
     scale = lax.rsqrt(square / feats + 1e-05)
 
+    wanted = column(targets[...], 0) - p * vocab
     top = jnp.full((slab, 1), -jnp.inf, f32)
     hit = jnp.zeros((slab, 1), f32)
     for j in range(n_lc):
@@ -301,9 +332,9 @@
         value = (own_lg[:, cols] + lg_rx[:, cols].astype(f32)) * scale
         own_lg[:, cols] = value
         top = jnp.maximum(top, jnp.max(value, axis=1, keepdims=True))
-        place = p * vocab + j * LC + lax.broadcasted_iota(jnp.int32, (slab, LC), 1)
+        place = j * LC + lax.broadcasted_iota(jnp.int32, (slab, LC), 1)
         hit = hit + jnp.sum(
-            jnp.where(place == targets[...], value, f32(0.0)), axis=1, keepdims=True
+            jnp.where(place == wanted, value, f32(0.0)), axis=1, keepdims=True
         )
     summed = jnp.zeros((slab, 1), f32)
     for j in range(n_lc):
@@ -328,7 +359,11 @@
     result = jnp.sum(hits, axis=0) - top_all - jnp.log(exp_total)
     lp_out[...] = jnp.broadcast_to(result, lp_out.shape)
 
-    for copy in [tok_x, w_x, tok_c, core_x, xm, xf] + rs + ag + fw + st:
+    for j in range(n_q):
+        core_x(j).wait_send()
+        for d in range(1, n_chip):
+            rs_copy(j, d).wait_send()
+    for copy in [tok_x, w_x, tok_c, xm, xf] + ag + fw + st:
         copy.wait_send()
 
     def hdone(j, carry):
@@ -349,9 +384,6 @@
     tokens, expert_ids, gate_values, targets, w_gate, w_up, w_down, norm_gain, lens_head
 ):
     slab, feats = tokens.shape
-    owner = lax.axis_index("expert")
-    weights = jnp.sum(jnp.where(expert_ids == owner, gate_values, f32(0.0)), axis=1)
-    weights = jnp.broadcast_to(weights[:, None], (slab, 128))
     wg = w_gate.reshape(feats, -1)
     wu = w_up.reshape(feats, -1)
     wd = w_down.reshape(w_down.shape[2], w_down.shape[3])
@@ -362,7 +394,7 @@
     n_hc, n_lc = hid // HC, vocab // LC
     dma = pltpu.SemaphoreType.DMA
     vmem = pl.BlockSpec(memory_space=pltpu.VMEM)
-    hbm = pl.BlockSpec(memory_space=pl.ANY)
+    hbm = pl.BlockSpec(memory_space=pltpu.HBM)
     flops = 2 * all_rows * (2 * feats * hid + 2 * hid * half + half * vocab)
     mixed, lp = pl.pallas_call(
         fused_kernel,
@@ -370,7 +402,7 @@
             jax.ShapeDtypeStruct((slab, feats), bf16),
             jax.ShapeDtypeStruct((8, 128), f32),
         ),
-        in_specs=[hbm, vmem, vmem, hbm, hbm, hbm, vmem, hbm],
+        in_specs=[hbm] * 9,
         out_specs=(vmem, vmem),
         scratch_shapes=[
             pltpu.VMEM((all_rows, feats), bf16),
@@ -392,11 +424,15 @@
             pltpu.VMEM((slab, vocab), bf16),
             pltpu.VMEM((slab, vocab), bf16),
             pltpu.VMEM((n_plane, 8, 128), f32),
-            dma((3,)), dma((n_hc,)), dma((n_hc,)),
+            pltpu.VMEM((2, slab), jnp.int32),
+            pltpu.VMEM((2, slab), f32),
+            pltpu.VMEM((1, slab), jnp.int32),
+            pltpu.VMEM((1, feats), f32),
+            dma((7,)), dma((n_hc,)), dma((n_hc,)),
             dma((3,)), dma((3,)),
             dma((2 * n_hc,)), dma((2 * n_hc,)),
-            dma, dma,
-            dma((n_chip - 1,)), dma((n_chip - 1,)),
+            dma((half // HC // 2,)), dma((half // HC // 2,)),
+            dma(((n_chip - 1) * (half // HC // 2),)), dma(((n_chip - 1) * (half // HC // 2),)),
             dma((n_chip - 1,)), dma((n_chip - 1,)),
             dma((n_chip,)), dma((n_chip,)),
             dma((2,)), dma((2,)),
@@ -404,12 +440,15 @@
             dma((n_plane - 1,)), dma((n_plane - 1,)),
         ],
         compiler_params=pltpu.CompilerParams(
-            collective_id=0, has_side_effects=True, vmem_limit_bytes=48 * 1024 * 1024
+            collective_id=0, has_side_effects=True, vmem_limit_bytes=63_060_000
         ),
         cost_estimate=pl.CostEstimate(
             flops=flops, bytes_accessed=4 * wg.size * 2, transcendentals=0
         ),
-    )(tokens, weights, targets[:, None], wg, wu, wd, norm_gain[None, :], lens_head)
+    )(
+        tokens, expert_ids.T, gate_values.T, targets[None, :], wg, wu, wd,
+        norm_gain[None, :], lens_head,
+    )
     return (mixed, lp[0, :slab])
 
 

time: 56.5 us -> 54 us (0.956)
  Pallas kernels: 51.1 us -> 50.2 us
  local copies, waits for them, and re-layouts: 3.78 us -> 2.95 us
  other arithmetic: 0.71 us -> 0 us
    pallas_call x1, Pallas kernels: 51.1 us -> 50.2 us  [per_device_fused(): pl.pallas_call(fused_kernel, out_shape=(jax.ShapeDtypeStruct((slab, feats...]
    broadcast_in_dim x2 -> x0, local copies, waits for them, and re-layouts: 0.82 us -> none  [the longest x1 0.75 us: per_device_fused(): targets[:, None]]
    reduce_sum x1 -> x0, other arithmetic: 0.71 us -> none  [per_device_fused(): jnp.sum(jnp.where(expert_ids == owner, gate_values, f32(0.0)), axis=1)]
    unnamed x5 -> x1, local copies, waits for them, and re-layouts: 2.45 us -> 1.77 us
    squeeze x1, local copies, waits for them, and re-layouts: 0.51 us -> 1.18 us  [per_device_fused(): return (mixed, lp[0, :slab])]
where the time goes in v3:
time: 54 us; the launch traced here: 53.8 us
  Pallas kernels  50.2 us (93%)
  local copies, waits for them, and re-layouts  2.95 us (5%)
  between operations  0.64 us (1%)
    pallas_call x1, Pallas kernels, per_device_fused(): pl.pallas_call(fused_kernel, out_shape=(jax.ShapeDtypeStruct((slab, feats...  50.2 us
    unnamed x1, local copies, waits for them, and re-layouts  1.77 us
    squeeze x1, local copies, waits for them, and re-layouts, per_device_fused(): return (mixed, lp[0, :slab])  1.18 us

profile of v3, /device:TPU:0, one launch (start us, length us, event | category | flops | bytes accessed | tf_op | source)
XLA Modules:
  0.0 53.8 jit_solution(8209553603870718387)
XLA Ops:
  0.6 50.2 %shard_map.104 = (bf16[64,3072]{1,0:T(8,128)(2,1)}, f32[8,128]{1,0:T(8,128)}) custom-call(bf16[64,3072]{1,0:T(8,128)(2,1)} %tok_hbm.1, s32[2,64]{1,0:T(2,128)} %bitcast.13, f32[2,64]{1,0:T(2,128)} %bitcast.14, s32[1,64]{1,0:T(1,128)} %bitcast.15, bf16[3072,1024]{1,0:T(8,128)(2,1)} %bitcast.9, bf16[3072,1024]{1,0:T(8,128)(2,1)} %bitcast.10, ...), custom_call_target="tpu_custom_call" | custom-call | flops 3221225472 | bytes 25165824 | tf_op jit(solution)/shard_map/pallas_call | solution.py:399
  50.9 1.2 %slice_bitcast_fusion = f32[64]{0:T(128)} fusion(f32[8,128]{1,0:T(8,128)} %get-tuple-element.5), kind=kLoop, calls=%fused_computation | loop fusion | bytes 512 | tf_op jit(solution)/shard_map/squeeze | solution.py:452
  52.1 1.8 %copy.12 = bf16[64,3072]{1,0:T(8,128)(2,1)} copy(bf16[64,3072]{1,0:T(8,128)(2,1)} %get-tuple-element.8) | data formatting | bytes 786432
